TPU v7x, 256 devices: a whole 4x4x8 slice. The times are simulated.
256 devices in a mesh: grp: 16 (over y, x), seq: 16 (over z, core).
Axes of the slice: x: 4, y: 4, z: 8, core: 2. Of those that a mesh axis runs over, the one named last changes fastest.
Arguments:
- inputs: bfloat16 [65536, 2560], P(('grp', 'seq')), may hold values from -0.03125 to 0.03125
- out_grad: bfloat16 [65536, 2560], P(('grp', 'seq')), may hold values from -6 to 6
- input_map: bfloat16 [65536, 128], P(('grp', 'seq')), may hold values from -0.09375 to 0.09375
- output_map: bfloat16 [65536, 128], P(('grp', 'seq')), may hold values from -0.09375 to 0.09375
- log_decay: float32 [40, 65536], P(None, ('grp', 'seq')), may hold values from -1 to 0, as said below
Outputs:
- grad_inputs: bfloat16 [65536, 2560], P(('grp', 'seq'))
- grad_input_map: bfloat16 [65536, 128], P(('grp', 'seq'))
- grad_output_map: bfloat16 [65536, 128], P(('grp', 'seq'))
- grad_decay: float32 [40, 65536], P(None, ('grp', 'seq'))
Inputs may be any that keep to these rules, and one draw needn't show every extreme that they name: log_decay is negative everywhere.
All inputs are finite; a program needn't handle non-finite values.
Results may differ from a plain program's by a relative error of at most 0.0081.
Values sent between devices are 32-bit elements; how exact they have to be, the bound alone decides.
A program may use at most 192 MiB of HBM per device.

v0:
```python
import jax
import jax.numpy as jnp
from jax import lax
from jax.sharding import PartitionSpec as P

STATE = 128
STRETCH = 256


def prefix_2(value, axis, join, neutral, backward):
    count, mine = (lax.axis_size(axis), lax.axis_index(axis))
    pieces = jax.tree.map(lambda part: lax.all_gather(part, axis), value)
    if backward:
        pieces = jax.tree.map(lambda part: part[::-1], pieces)
        mine = count - 1 - mine
    total = jax.tree.map(
        lambda part, zero: jnp.full_like(part, 0) + jnp.asarray(zero, part.dtype), value, neutral
    )

    def lap(position, total):
        longer = join(total, jax.tree.map(lambda part: part[position], pieces))
        return jax.tree.map(lambda new, old: jnp.where(position < mine, new, old), longer, total)

    return lax.fori_loop(0, count - 1, lap, total)


def weigh(values, grads, rates):
    cumulative = jnp.cumsum(rates, axis=1)
    block_decay = cumulative[:, -1]
    decay_tail = jnp.exp(block_decay[:, None] - cumulative)
    decay_lead = jnp.exp(cumulative)
    inputs_tail = (values.astype(jnp.float32) * decay_tail.T[:, :, None]).astype(jnp.bfloat16)
    grads_lead = (grads.astype(jnp.float32) * decay_lead.T[:, :, None]).astype(jnp.bfloat16)
    return (cumulative, block_decay, decay_tail, decay_lead, inputs_tail, grads_lead)


def block_summary(values, grads, write_map, read_map, rates):
    cumulative, block_decay, decay_tail, decay_lead, inputs_tail, grads_lead = weigh(
        values, grads, rates
    )
    own_state = jnp.einsum(
        "khp,kn->hpn", inputs_tail, write_map, preferred_element_type=jnp.float32
    )
    own_back = jnp.einsum("khp,kn->hpn", grads_lead, read_map, preferred_element_type=jnp.float32)
    return (block_decay, own_state, own_back)


def block_intra(values, grads, write_map, read_map, rates):
    head_count = rates.shape[0]
    length = rates.shape[1]
    head_size = values.shape[2]
    group_size = 8
    group_count = head_count // group_size
    cumulative = jnp.cumsum(rates, axis=1)
    row_ids = lax.broadcasted_iota(jnp.int32, (length, length), 0)
    col_ids = lax.broadcasted_iota(jnp.int32, (length, length), 1)
    causal = (row_ids >= col_ids)[None]
    scores = jnp.dot(read_map, write_map.T, preferred_element_type=jnp.float32)
    grouped_values = values.reshape(length, group_count, group_size, head_size).transpose(
        1, 0, 2, 3
    )
    grouped_grads = grads.reshape(length, group_count, group_size, head_size).transpose(1, 0, 2, 3)
    grouped_cumul = cumulative.reshape(group_count, group_size, length)

    def one_group(carry, item):
        group_values, group_grads, group_cumul = item
        log_gap = group_cumul[:, :, None] - group_cumul[:, None, :]
        decay = jnp.where(causal, jnp.exp(jnp.where(causal, log_gap, 0.0)), 0.0)
        mixing = (scores[None] * decay).astype(jnp.bfloat16)
        y_part = jnp.einsum(
            "hij,jhp->ihp", mixing, group_values, preferred_element_type=jnp.float32
        )
        dx_part = jnp.einsum(
            "hij,ihp->jhp", mixing, group_grads, preferred_element_type=jnp.float32
        )
        pair_dots = jnp.einsum(
            "ihp,jhp->hij", group_values, group_grads, preferred_element_type=jnp.float32
        )
        carry = carry + jnp.sum(pair_dots * jnp.swapaxes(decay, 1, 2), axis=0)
        return (carry, (y_part, dx_part))

    summed, (y_parts, dx_parts) = lax.scan(
        one_group,
        jnp.zeros((length, length), jnp.float32),
        (grouped_values, grouped_grads, grouped_cumul),
    )
    y_intra = y_parts.transpose(1, 0, 2, 3).reshape(length, head_count, head_size)
    dx_intra = dx_parts.transpose(1, 0, 2, 3).reshape(length, head_count, head_size)
    head_sum = summed.astype(jnp.bfloat16)
    db_intra = jnp.dot(head_sum, read_map, preferred_element_type=jnp.float32)
    dc_intra = jnp.dot(head_sum.T, write_map, preferred_element_type=jnp.float32)
    return (y_intra, dx_intra, db_intra, dc_intra)


def block_final(
    values,
    grads,
    write_map,
    read_map,
    rates,
    y_intra,
    dx_intra,
    db_intra,
    dc_intra,
    state_in,
    back_in,
):
    cumulative, block_decay, decay_tail, decay_lead, inputs_tail, grads_lead = weigh(
        values, grads, rates
    )
    state_half = state_in.astype(jnp.bfloat16)
    back_half = back_in.astype(jnp.bfloat16)
    outputs_full = (
        y_intra
        + jnp.einsum("kn,hpn->khp", read_map, state_half, preferred_element_type=jnp.float32)
        * decay_lead.T[:, :, None]
    )
    grad_full = (
        dx_intra
        + jnp.einsum("kn,hpn->khp", write_map, back_half, preferred_element_type=jnp.float32)
        * decay_tail.T[:, :, None]
    )
    grad_write = db_intra + jnp.einsum(
        "khp,hpn->kn", inputs_tail, back_half, preferred_element_type=jnp.float32
    )
    grad_read = dc_intra + jnp.einsum(
        "khp,hpn->kn", grads_lead, state_half, preferred_element_type=jnp.float32
    )
    change = jnp.sum(
        grads.astype(jnp.float32) * outputs_full - values.astype(jnp.float32) * grad_full, axis=2
    ).T
    return (
        grad_full.astype(jnp.bfloat16),
        grad_write.astype(jnp.bfloat16),
        grad_read.astype(jnp.bfloat16),
        change,
    )


def apply_first(first_part, second_part):
    return (
        first_part[0] * second_part[0],
        second_part[0][:, None, None] * first_part[1] + second_part[1],
    )


def per_device(inputs, out_grad, input_map, output_map, log_decay):
    head_count = log_decay.shape[0]
    tokens = inputs.shape[0]
    head_size = inputs.shape[1] // head_count
    blocks = tokens // STRETCH
    parts = (
        inputs.reshape(blocks, STRETCH, head_count, head_size),
        out_grad.reshape(blocks, STRETCH, head_count, head_size),
        input_map.reshape(blocks, STRETCH, STATE),
        output_map.reshape(blocks, STRETCH, STATE),
        log_decay.reshape(head_count, blocks, STRETCH).transpose(1, 0, 2),
    )
    decays, own_states, own_backs = lax.map(lambda pieces: block_summary(*pieces), parts)
    empty_state = jnp.zeros((head_count, head_size, STATE), jnp.float32)

    def forward(running, item):
        block_decay, own_state = item
        return (jnp.exp(block_decay)[:, None, None] * running + own_state, running)

    def backward(running, item):
        block_decay, own_back = item
        return (jnp.exp(block_decay)[:, None, None] * running + own_back, running)

    shard_state, shard_local_states = lax.scan(forward, empty_state, (decays, own_states))
    shard_back, local_backs = lax.scan(backward, empty_state, (decays, own_backs), reverse=True)
    shard_log = jnp.sum(decays, axis=0)
    shard_decay = jnp.exp(shard_log)
    identity = (jnp.ones((head_count,), jnp.float32), empty_state)
    intra = lax.map(lambda pieces: block_intra(*pieces), parts)
    prefix = prefix_2((shard_decay, shard_state), "seq", apply_first, identity, False)
    trailing_sum = prefix_2((shard_decay, shard_back), "seq", apply_first, identity, True)
    whole_up = apply_first(prefix, (shard_decay, shard_state))
    whole_down = apply_first(trailing_sum, (shard_decay, shard_back))
    position = lax.axis_index("seq")
    mask_last = (position == lax.axis_size("seq") - 1).astype(jnp.float32)
    mask_first = (position == 0).astype(jnp.float32)
    group_totals = lax.psum(
        (
            whole_up[0] * mask_last,
            whole_up[1] * mask_last,
            whole_down[0] * mask_first,
            whole_down[1] * mask_first,
        ),
        "seq",
    )
    outer_up = prefix_2((group_totals[0], group_totals[1]), "grp", apply_first, identity, False)
    outer_down = prefix_2((group_totals[2], group_totals[3]), "grp", apply_first, identity, True)
    incoming = apply_first(outer_up, prefix)[1]
    outgoing = apply_first(outer_down, trailing_sum)[1]
    running_sum = jnp.cumsum(decays, axis=0)
    before = running_sum - decays
    after = shard_log[None, :] - running_sum
    states_in = shard_local_states + jnp.exp(before)[:, :, None, None] * incoming[None]
    backs_in = local_backs + jnp.exp(after)[:, :, None, None] * outgoing[None]

    def finish(item):
        pieces, intra_part, state_in, back_in = item
        return block_final(*pieces, *intra_part, state_in, back_in)

    grad_values, grad_write, grad_read, change = lax.map(
        finish, (parts, intra, states_in, backs_in)
    )
    change = change.transpose(1, 0, 2).reshape(head_count, tokens)
    suffix_local = jnp.cumsum(change[:, ::-1], axis=1)[:, ::-1]
    shard_total = suffix_local[:, 0]
    every_total = lax.all_gather(shard_total[None, :], ("grp", "seq"), axis=0, tiled=True)
    flat_position = lax.axis_index(("grp", "seq"))
    shard_ranks = lax.broadcasted_iota(jnp.int32, every_total.shape, 0)
    later_sum = jnp.sum(jnp.where(shard_ranks > flat_position, every_total, 0.0), axis=0)
    grad_decay = suffix_local + later_sum[:, None]
    return (
        grad_values.reshape(tokens, head_count * head_size),
        grad_write.reshape(tokens, STATE),
        grad_read.reshape(tokens, STATE),
        grad_decay,
    )


def solution(mesh):
    in_specs = (
        P(("grp", "seq"), None),
        P(("grp", "seq"), None),
        P(("grp", "seq"), None),
        P(("grp", "seq"), None),
        P(None, ("grp", "seq")),
    )
    out_specs = (
        P(("grp", "seq"), None),
        P(("grp", "seq"), None),
        P(("grp", "seq"), None),
        P(None, ("grp", "seq")),
    )
    return jax.shard_map(
        per_device, mesh=mesh, in_specs=in_specs, out_specs=out_specs, check_vma=False
    )
```

profile of v0, /device:TPU:1, one launch (start us, length us, event | category | flops | bytes accessed | tf_op | source)
XLA Modules:
  0.0 815.2 jit_solution(6809882130376088572)
XLA Ops:
  18.2 28.9 %all-reduce = f32[640]{0:T(1024)S(1)} all-reduce(f32[640]{0:T(1024)S(1)} %dynamic-update-slice), channel_id=2, replica_groups=mesh['grp'=16,'seq'=16] {'seq'}, use_global_device_ids=true, to_apply=%add | all-reduce | flops 640 | bytes 5120
  47.2 85.1 %all-gather.15.cloned.1.call-done = f32[640,64,128]{2,1,0:T(8,128)} async-done(((f32[40,64,128]{2,1,0:T(8,128)}), f32[640,64,128]{2,1,0:T(8,128)}) %all-gather.15.cloned.1.call-update) | async-done | bytes 20971536 | tf_op jit(solution)/shard_map/all_gather | solution.py:12
  132.3 16.6 %rev.17 = f32[16,40,64,128]{3,2,1,0:T(8,128)} reverse(f32[16,40,64,128]{3,2,1,0:T(8,128)} %bitcast.199), dimensions={0} | reverse | bytes 41943040 | tf_op jit(solution)/shard_map/rev | solution.py:14
  148.9 25.6 %while.59 = (s32[]{:T(128)}, f32[40]{0:T(128)S(1)}, f32[40,64,128]{2,1,0:T(8,128)S(1)}, s32[]{:T(128)}, f32[16,40]{1,0:T(8,128)S(1)}, /*index=5*/f32[16,40,64,128]{3,2,1,0:T(8,128)}, s32[]{:T(128)}, s32[]{:T(128)}) while((s32[]{:T(128)}, f32[40]{0:T(128)S(1)}, f32[40,64,128]{2,1,0:T(8,128)S(1)}, s32[]{:T(128)}, ...), condition=%wide.region_6.7_spmd.clone, body=%wide.region_5.6_spmd.clone.sunk | while | flops 1310844 | bytes 3933075 | solution.py:24
  174.4 74.0 %all-gather.17.cloned.1.call-done = f32[640,64,128]{2,1,0:T(8,128)} async-done(((f32[40,64,128]{2,1,0:T(8,128)}), f32[640,64,128]{2,1,0:T(8,128)}) %all-gather.17.cloned.1.call-update) | async-done | bytes 20971536 | tf_op jit(solution)/shard_map/all_gather | solution.py:12
  248.4 25.0 %while.61 = (s32[]{:T(128)}, f32[40]{0:T(128)S(1)}, f32[40,64,128]{2,1,0:T(8,128)S(1)}, s32[]{:T(128)}, f32[16,40]{1,0:T(8,128)S(1)}, /*index=5*/f32[16,40,64,128]{3,2,1,0:T(8,128)}, s32[]{:T(128)}, s32[]{:T(128)}) while((s32[]{:T(128)}, f32[40]{0:T(128)S(1)}, f32[40,64,128]{2,1,0:T(8,128)S(1)}, s32[]{:T(128)}, ...), condition=%wide.region_12.13_spmd.clone, body=%wide.region_11.12_spmd.clone.sunk | while | flops 1310844 | bytes 3933075 | solution.py:24
  273.4 3.6 multiply_bitcast_fusion
  277.0 114.7 %all-reduce.6.cloned.1.call-done = (f32[1,40,64,128]{3,2,1,0:T(8,128)}, f32[1,40,64,128]{3,2,1,0:T(8,128)}) async-done(((f32[1,40,64,128]{3,2,1,0:T(8,128)}, f32[1,40,64,128]{3,2,1,0:T(8,128)}), (f32[1,40,64,128]{3,2,1,0:T(8,128)}, f32[1,40,64,128]{3,2,1,0:T(8,128)})) %all-reduce.6.cloned.1.call-update) | async-done | bytes 2621456 | tf_op jit(solution)/shard_map/psum | solution.py:183
  392.4 3.7 fusion.26
  397.2 36.5 %while.63 = (s32[]{:T(128)}, f32[256,256]{1,0:T(8,128)S(1)}, f32[5,256,8,64]{1,3,2,0:T(8,128)}, f32[5,256,8,64]{1,3,2,0:T(8,128)}, bf16[5,256,8,64]{1,3,2,0:T(8,...) while((s32[]{:T(128)}, f32[256,256]{1,0:T(8,128)S(1)}, ...), condition=%wide.region_4.5_spmd.clone.clone, body=%wide.region_2.4_spmd.clone.clone.sunk | while | flops 209387520 | bytes 5246095 | solution.py:82
  399.3 2.6 fusion.79
  402.0 2.5 fusion.80
  406.6 2.7 fusion.79
  409.3 2.5 fusion.80
  414.0 2.6 fusion.79
  416.6 2.5 fusion.80
  419.1 1.8 multiply_reduce_fusion.2
  421.2 2.6 fusion.79
  423.9 2.5 fusion.80
  426.4 1.8 multiply_reduce_fusion.2
  428.5 2.6 fusion.79
  431.1 2.5 fusion.80
  433.6 24.4 %all-reduce.2 = (f32[1,40]{1,0:T(1,128)S(1)}, f32[1,40]{1,0:T(1,128)S(1)}) all-reduce(f32[1,40]{1,0:T(1,128)S(1)} %get-tuple-element.837, f32[1,40]{1,0:T(1,128)S(1)} %get-tuple-element.836), channel_id=1, replica_groups=mesh['grp'=16,'seq'=16] {'seq'}, use_global_device_ids=true, to_apply=%region_7.8 | all-reduce | flops 80 | bytes 640 | tf_op jit(solution)/shard_map/psum | solution.py:183
  458.1 18.7 %all-gather.4 = f32[16,1,40]{2,1,0:T(1,128)S(1)} all-gather(f32[1,1,40]{2,1,0:T(1,128)S(1)} %bitcast.214), channel_id=1, replica_groups=mesh['grp'=16,'seq'=16] {'grp'}, dimensions={0}, use_global_device_ids=true | all-gather | bytes 2720 | tf_op jit(solution)/shard_map/all_gather | solution.py:12
  476.8 16.9 %all-gather.5 = f32[16,1,40]{2,1,0:T(1,128)S(1)} all-gather(f32[1,1,40]{2,1,0:T(1,128)S(1)} %bitcast.213), channel_id=1, replica_groups=mesh['grp'=16,'seq'=16] {'grp'}, dimensions={0}, use_global_device_ids=true | all-gather | bytes 2720 | tf_op jit(solution)/shard_map/all_gather | solution.py:12
  493.7 38.8 %all-gather.11.cloned.1.call-done = f32[16,40,64,128]{3,2,1,0:T(8,128)} async-done(((f32[1,40,64,128]{3,2,1,0:T(8,128)}), f32[16,40,64,128]{3,2,1,0:T(8,128)}) %all-gather.11.cloned.1.call-update) | async-done | bytes 20971536 | tf_op jit(solution)/shard_map/all_gather | solution.py:12
  532.5 16.4 %rev.19 = f32[16,40,64,128]{3,2,1,0:T(8,128)} reverse(f32[16,40,64,128]{3,2,1,0:T(8,128)} %all-gather.11.cloned.1.call-done), dimensions={0} | reverse | bytes 41943040 | tf_op jit(solution)/shard_map/rev | solution.py:14
  548.9 47.0 %while.60 = (s32[]{:T(128)}, f32[40,64,128]{2,1,0:T(8,128)}, s32[]{:T(128)}, f32[16,40]{1,0:T(8,128)S(1)}, f32[16,40,64,128]{3,2,1,0:T(8,128)}, /*index=5*/s32[]{:T(128)}, s32[]{:T(128)}) while((s32[]{:T(128)}, f32[40,64,128]{2,1,0:T(8,128)}, s32[]{:T(128)}, f32[16,40]{1,0:T(8,128)S(1)}, f32[16,40,64,128]{3,2,1,0:T(8,128)}, ...), condition=%wide.region_10.11_spmd.clone, body=%wide.region_9.10_spmd.clone.sunk | while | flops 1310724 | bytes 3932745 | solution.py:24
  548.9 3.0 fusion.70
  551.8 3.1 fusion.70
  554.9 3.1 fusion.70
  558.0 3.1 fusion.70
  561.1 3.1 fusion.70
  564.3 3.1 fusion.70
  567.5 3.1 fusion.70
  570.5 3.1 fusion.70
  573.6 3.1 fusion.70
  576.7 3.1 fusion.70
  579.8 3.1 fusion.70
  582.9 3.1 fusion.70
  585.9 3.7 fusion.70
  589.7 3.1 fusion.70
  592.8 3.1 fusion.70
  595.8 76.2 %all-gather.13.cloned.1.call-done = f32[16,40,64,128]{3,2,1,0:T(8,128)} async-done(((f32[1,40,64,128]{3,2,1,0:T(8,128)}), f32[16,40,64,128]{3,2,1,0:T(8,128)}) %all-gather.13.cloned.1.call-update) | async-done | bytes 20971536 | tf_op jit(solution)/shard_map/all_gather | solution.py:12
  672.1 44.6 %while.62 = (s32[]{:T(128)}, f32[40,64,128]{2,1,0:T(8,128)}, s32[]{:T(128)}, f32[16,40]{1,0:T(8,128)S(1)}, f32[16,40,64,128]{3,2,1,0:T(8,128)}, /*index=5*/s32[]{:T(128)}, s32[]{:T(128)}) while((s32[]{:T(128)}, f32[40,64,128]{2,1,0:T(8,128)}, s32[]{:T(128)}, f32[16,40]{1,0:T(8,128)S(1)}, f32[16,40,64,128]{3,2,1,0:T(8,128)}, ...), condition=%wide.region_16.17_spmd.clone, body=%wide.region_15.16_spmd.clone.sunk | while | flops 1310724 | bytes 3932745 | solution.py:24
  672.1 2.6 fusion.72
  674.7 3.0 fusion.72
  677.7 3.0 fusion.72
  680.7 3.0 fusion.72
  683.7 3.0 fusion.72
  686.7 3.0 fusion.72
  689.7 3.0 fusion.72
  692.7 3.0 fusion.72
  695.7 3.0 fusion.72
  698.7 3.0 fusion.72
  701.7 3.0 fusion.72
  704.7 3.0 fusion.72
  707.7 3.0 fusion.72
  710.7 3.0 fusion.72
  713.7 3.0 fusion.72
  716.7 2.2 multiply_convert_fusion.7
  718.9 3.8 fusion.38
  725.5 76.3 %all-reduce.1 = f32[10240]{0:T(1024)S(1)} all-reduce(f32[10240]{0:T(1024)S(1)} %dynamic-update-slice.1), channel_id=5, replica_groups=mesh['grp'=16,'seq'=16] {'grp','seq'}, use_global_device_ids=true, to_apply=%add.1 | all-reduce | flops 10240 | bytes 81920
  801.9 2.1 convolution_bitcast_fusion.2
  (219 shorter events, 76.3 us)
Async XLA Ops:
  7.2 7.2 copy-start
  7.2 125.1 %all-gather.15.cloned.1.call-start = ((), (), s32[]{:S(2)}) async-start(), calls=%async_computation.2 | async-start | bytes 22282240 | tf_op jit(solution)/shard_map/all_gather | solution.py:12
  9.2 1.7 copy-start.12
  10.8 1.6 copy-start.1
  12.5 1.3 copy-start.10
  12.5 236.0 %all-gather.17.cloned.1.call-start = ((), (), s32[]{:S(2)}) async-start(), calls=%async_computation.3 | async-start | bytes 22282240 | tf_op jit(solution)/shard_map/all_gather | solution.py:12
  14.4 1.6 copy-start.3
  16.0 0.7 copy-start.14
  16.0 375.7 %all-reduce.6.cloned.1.call-start = ((), (), s32[]{:S(2)}) async-start(), calls=%async_computation.4 | async-start | bytes 5242880 | tf_op jit(solution)/shard_map/psum | solution.py:183
  277.0 255.5 %all-gather.11.cloned.1.call-start = ((), (), s32[]{:S(2)}) async-start(), calls=%async_computation | async-start | bytes 22282240 | tf_op jit(solution)/shard_map/all_gather | solution.py:12
  391.7 280.4 %all-gather.13.cloned.1.call-start = ((), (), s32[]{:S(2)}) async-start(), calls=%async_computation.1 | async-start | bytes 22282240 | tf_op jit(solution)/shard_map/all_gather | solution.py:12
  399.3 2.6 copy-start.13
  406.6 2.7 copy-start.13
  414.0 2.6 copy-start.13
  421.2 2.6 copy-start.13
  428.5 2.6 copy-start.13
  718.9 3.9 copy-start.8
  718.9 3.9 copy-start.6
  718.9 3.8 copy-start.2
  718.9 3.8 copy-start.4
  718.9 3.8 copy-start.7
  801.8 2.3 copy-start.9
  801.9 2.2 copy-start.11
  804.1 2.2 copy-start.5
Sparse Core Ops, SparseCore 0:
  12.6 119.6 all-gather.14
  134.7 113.6 all-gather.16
  277.1 114.5 all-reduce.5
  394.0 138.4 all-gather.10
  534.8 137.2 all-gather.12
where the time goes:
time: 818 us; the launch traced here: 815 us
  waiting for transfers between devices  389 us (48%)
  blocking collectives  165 us (20%)
  other arithmetic  154 us (19%)
  matrix products  48.1 us (6%)
  local copies, waits for them, and re-layouts  42.8 us (5%)
  between operations  14.8 us (2%)
    all_gather x4, waiting for transfers between devices, prefix_2(): pieces = jax.tree.map(lambda part: lax.all_gather(part, axis), value)  274 us
    select_n x90, other arithmetic, lap(): jnp.where(position < mine, new, old)  141 us
    psum x1, waiting for transfers between devices, per_device(): lax.psum((whole_up[0] * mask_last, whole_up[1] * mask_last, whole_down[0]...  115 us
    unnamed x2, blocking collectives  105 us
    all_gather x2, blocking collectives, prefix_2(): pieces = jax.tree.map(lambda part: lax.all_gather(part, axis), value)  35.6 us
    rev x4, local copies, waits for them, and re-layouts, prefix_2(): pieces = jax.tree.map(lambda part: part[::-1], pieces)  33 us
    psum x1, blocking collectives, per_device(): lax.psum((whole_up[0] * mask_last, whole_up[1] * mask_last, whole_down[0]...  24.4 us
  transfers between devices with their start and end apart: 5, of which 5 were waited for; matrix products, arithmetic and copies ran while one was open for 18% of the time, Pallas kernels for 0%

commit v1 on v0

v1 whole, which is shorter than its diff:
```python
import jax
import jax.numpy as jnp
from jax import lax
from jax.experimental import pallas as pl
from jax.experimental.pallas import tpu as pltpu
from jax.sharding import PartitionSpec as P

MESH = pl.DeviceIdType.MESH
HIGH = lax.Precision.HIGHEST
F32 = jnp.float32
BF16 = jnp.bfloat16
LIMIT = 56 * 2**20

T = 256
HEADS = 40
N = 128
WIDE = 2560
HALF = WIDE // 2
Z, CORES, GROUPS = 8, 2, 16
SLICE = N // Z


def nn(a, b, precision=None):
    return lax.dot_general(
        a, b, (((1,), (0,)), ((), ())), precision=precision, preferred_element_type=F32
    )


def nt(a, b, precision=None):
    return lax.dot_general(
        a, b, (((1,), (1,)), ((), ())), precision=precision, preferred_element_type=F32
    )


def tn(a, b, precision=None):
    return lax.dot_general(
        a, b, (((0,), (0,)), ((), ())), precision=precision, preferred_element_type=F32
    )


def iota(shape, dim):
    return lax.broadcasted_iota(jnp.int32, shape, dim)


def running(rates):
    padded = jnp.concatenate([rates, jnp.zeros((N - HEADS, T), F32)], axis=0)
    upto = (iota((T, T), 1) <= iota((T, T), 0)).astype(F32)
    return padded, nt(upto, padded, HIGH)


def own(v_ref, g_ref, w_ref, r_ref, a_ref, vt_ref, gl_ref, of_ref, ob_ref, log_ref):
    _, cum = running(a_ref[...])
    block = cum[T - 1 : T, :]
    log_ref[...] = jnp.broadcast_to(block, (8, N))
    tail, lead = jnp.exp(block - cum), jnp.exp(cum)
    left = iota((T, N), 1) < N // 2
    w_t, r_t = w_ref[...].T, r_ref[...].T
    for i in range(HEADS // 2):
        at = slice(N * i, N * i + N)
        a, b = 2 * i, 2 * i + 1
        tails = jnp.where(left, tail[:, a : a + 1], tail[:, b : b + 1])
        leads = jnp.where(left, lead[:, a : a + 1], lead[:, b : b + 1])
        vt = (v_ref[:, at].astype(F32) * tails).astype(BF16)
        gl = (g_ref[:, at].astype(F32) * leads).astype(BF16)
        vt_ref[:, at] = vt
        gl_ref[:, at] = gl
        c, lanes = divmod(N * i, HALF)
        of_ref[c, :, lanes : lanes + N] = nn(w_t, vt)
        ob_ref[c, :, lanes : lanes + N] = nn(r_t, gl)


def exchange(
    of, ob, log, sf, sb,
    logs, glogs, xf, xb, cf, cb, uf, ub, pf, pb, tf, tb, df, db, kf, kb, yf, yb,
    wz, ez, fz, ex, wg,
    log_s, log_r, glog_s, glog_r, x_s, x_r, u_s, u_r, t_s, t_r, d_s, d_r,
):
    g, s = lax.axis_index("grp"), lax.axis_index("seq")
    z, c = s // CORES, s % CORES
    other = (g, z * CORES + 1 - c)

    def copy(src, dst, send, recv, device):
        return pltpu.make_async_remote_copy(
            src_ref=src,
            dst_ref=dst,
            send_sem=send,
            recv_sem=recv,
            device_id=device,
            device_id_type=MESH,
        )

    def over(count, mine, step):
        def lap(i, carry):
            step(lax.rem(mine + i, count))
            return carry

        lax.fori_loop(1, count, lap, 0)

    def rows(j):
        return pl.ds(pl.multiple_of(j * SLICE, SLICE), SLICE)

    barrier = pltpu.get_barrier_semaphore()

    def greet(device):
        pl.semaphore_signal(barrier, inc=1, device_id=device, device_id_type=MESH)

    over(Z * CORES, s, lambda k: greet((g, k)))
    over(GROUPS, g, lambda k: greet((k, s)))
    pl.semaphore_wait(barrier, Z * CORES - 1 + GROUPS - 1)

    logs[s] = log[...]

    def log_copy(k):
        return copy(logs.at[s], logs.at[s], log_s.at[k], log_r.at[s], (g, k))

    def log_here(k):
        return copy(logs.at[k], logs.at[k], log_s.at[k], log_r.at[k], (g, k))

    over(Z * CORES, s, lambda k: log_copy(k).start())
    up_f = copy(of.at[1 - c], xf, x_s.at[0], x_r.at[0], other)
    up_b = copy(ob.at[1 - c], xb, x_s.at[1], x_r.at[1], other)
    up_f.start()
    up_b.start()
    over(Z * CORES, s, lambda k: log_here(k).wait_recv())

    blocks = jnp.max(logs[...], axis=1)
    glogs[g] = jnp.broadcast_to(jnp.sum(blocks, axis=0, keepdims=True), (8, N))

    def glog_copy(k):
        return copy(glogs.at[g], glogs.at[g], glog_s.at[k], glog_r.at[g], (k, s))

    def glog_here(k):
        return copy(glogs.at[k], glogs.at[k], glog_s.at[k], glog_r.at[k], (k, s))

    over(GROUPS, g, lambda k: glog_copy(k).start())

    spread = (iota((N, HALF), 0) == iota((N, HALF), 1) // 64 + c * (HEADS // 2)).astype(F32)
    wide = nn(blocks, spread, HIGH)
    chip_of, place = iota((Z, Z * CORES), 1) // CORES, iota((Z, Z * CORES), 0)
    wz[...] = jnp.exp(nn((chip_of == place).astype(F32), wide, HIGH))
    ez[...] = jnp.exp(nn((chip_of < place).astype(F32), wide, HIGH))
    fz[...] = jnp.exp(nn((chip_of > place).astype(F32), wide, HIGH))
    mine = (iota((Z, Z * CORES), 1) == place + z * CORES).astype(F32)
    ex[...] = jnp.exp(nn(mine, wide, HIGH))
    first, second = ex[0:1, :], ex[1:2, :]
    one = jnp.ones_like(first)
    is_first = c == 0

    def slices_up(way, own_ref, theirs, chip, up, a, b):
        def put(j):
            chip[rows(j), :] = a * own_ref[c, rows(j), :] + b * theirs[rows(j), :]

        def send(j):
            put(j)
            copy(chip.at[rows(j)], up.at[z], u_s.at[way, j], u_r.at[way, z], (g, j * CORES + c)).start()

        over(Z, z, send)
        put(z)
        up[z] = chip[rows(z), :]

    up_f.wait_recv()
    slices_up(
        0, of, xf, cf, uf, jnp.where(is_first, second, one), jnp.where(is_first, one, second)
    )
    up_b.wait_recv()
    slices_up(1, ob, xb, cb, ub, jnp.where(is_first, one, first), jnp.where(is_first, first, one))

    def up_here(way, chip, up, j):
        return copy(chip.at[rows(j)], up.at[j], u_s.at[way, j], u_r.at[way, j], (g, j * CORES + c))

    def total_copy(way, total, k):
        return copy(total.at[g], total.at[g], t_s.at[way, k], t_r.at[way, g], (k, s))

    def total_here(way, total, k):
        return copy(total.at[k], total.at[k], t_s.at[way, k], t_r.at[way, k], (k, s))

    def ring(way, chip, up, part, total, order):
        over(Z, z, lambda j: up_here(way, chip, up, j).wait_recv())
        state = jnp.zeros((SLICE, HALF), F32)
        for j in order:
            part[j] = state
            state = wz[j : j + 1, :] * state + up[j]
        total[g] = state
        over(GROUPS, g, lambda k: total_copy(way, total, k).start())

    ring(0, cf, uf, pf, tf, range(Z))
    over(GROUPS, g, lambda k: glog_here(k).wait_recv())
    wg[...] = jnp.exp(nn(jnp.max(glogs[...], axis=1), spread, HIGH))
    ring(1, cb, ub, pb, tb, range(Z - 1, -1, -1))

    def down_copy(way, part, down, j):
        return copy(part.at[j], down.at[rows(z)], d_s.at[way, j], d_r.at[way, z], (g, j * CORES + c))

    def down_here(way, part, down, j):
        return copy(part.at[j], down.at[rows(j)], d_s.at[way, j], d_r.at[way, j], (g, j * CORES + c))

    def groups(way, part, total, down, decay, count, pick):
        over(GROUPS, g, lambda k: total_here(way, total, k).wait_recv())

        def lap(i, state):
            k = pick(i)
            return wg[pl.ds(k, 1), :] * state + total[k]

        state = lax.fori_loop(0, count, lap, jnp.zeros((SLICE, HALF), F32))

        def send(j):
            part[j] += decay[pl.ds(j, 1), :] * state
            down_copy(way, part, down, j).start()

        over(Z, z, send)
        down[rows(z), :] = part[z] + decay[pl.ds(z, 1), :] * state

    groups(0, pf, tf, df, ez, g, lambda i: i)
    groups(1, pb, tb, db, fz, GROUPS - 1 - g, lambda i: GROUPS - 1 - i)

    over(Z, z, lambda j: down_here(0, pf, df, j).wait_recv())
    out_f = copy(kf, yf, x_s.at[2], x_r.at[2], other)

    @pl.when(is_first)
    def _():
        kf[...] = first * df[...] + of[c]
        out_f.start()
        sf[c] = df[...]

    @pl.when(jnp.logical_not(is_first))
    def _():
        kf[...] = df[...]
        out_f.start()
        sf[c] = first * df[...] + xf[...]

    over(Z, z, lambda j: down_here(1, pb, db, j).wait_recv())
    out_b = copy(kb, yb, x_s.at[3], x_r.at[3], other)

    @pl.when(is_first)
    def _():
        kb[...] = db[...]
        out_b.start()
        sb[c] = second * db[...] + xb[...]

    @pl.when(jnp.logical_not(is_first))
    def _():
        kb[...] = second * db[...] + ob[c]
        out_b.start()
        sb[c] = db[...]

    out_f.wait_recv()
    sf[1 - c] = yf[...]
    out_b.wait_recv()
    sb[1 - c] = yb[...]

    over(Z * CORES, s, lambda k: log_copy(k).wait_send())
    over(GROUPS, g, lambda k: glog_copy(k).wait_send())
    for way, chip, up, part, total, down in ((0, cf, uf, pf, tf, df), (1, cb, ub, pb, tb, db)):
        over(Z, z, lambda j: up_here(way, chip, up, j).wait_send())
        over(GROUPS, g, lambda k: total_copy(way, total, k).wait_send())
        over(Z, z, lambda j: down_copy(way, part, down, j).wait_send())
    for each in (up_f, up_b, out_f, out_b):
        each.wait_send()


def finish(
    v_ref, g_ref, w_ref, r_ref, a_ref, vt_ref, gl_ref, of_ref, sf_ref, sb_ref,
    dv_ref, dw_ref, dr_ref, da_ref,
):
    padded, cum = running(a_ref[...])
    upto = (iota((T, T), 0) <= iota((T, T), 1)).astype(F32)
    cum_rows = nn(padded, upto, HIGH)
    block = cum[T - 1 : T, :]
    tail, lead = jnp.exp(block - cum), jnp.exp(cum)
    causal = iota((T, T), 0) >= iota((T, T), 1)
    left = iota((T, N), 1) < N // 2
    left_row = left[0:1, :]
    w, r = w_ref[...], r_ref[...]
    scores = nt(r, w)
    summed = jnp.zeros((T, T), F32)
    change = jnp.zeros((T, N), F32)
    later = jnp.zeros((1, N), F32)
    dw = jnp.zeros((T, N), F32)
    dr = jnp.zeros((T, N), F32)
    bd = jnp.exp(block)
    for i in range(HEADS // 2):
        at = slice(N * i, N * i + N)
        c, lanes = divmod(N * i, HALF)
        within = slice(lanes, lanes + N)
        heads = (2 * i, 2 * i + 1)
        v, g = v_ref[:, at], g_ref[:, at]
        y_two, dx_two = [], []
        for k, h in enumerate(heads):
            gap = cum[:, h : h + 1] - cum_rows[h : h + 1, :]
            decay = jnp.exp(jnp.where(causal, gap, -jnp.inf))
            mixing = (scores * decay).astype(BF16)
            y_two.append(nn(mixing, v))
            dx_two.append(tn(mixing, g))
            one = jnp.where(left if k == 0 else jnp.logical_not(left), g, jnp.zeros_like(g))
            summed = summed + nt(one, v) * decay
        a, b = heads
        tails = jnp.where(left, tail[:, a : a + 1], tail[:, b : b + 1])
        leads = jnp.where(left, lead[:, a : a + 1], lead[:, b : b + 1])
        state, back = sf_ref[c, :, within], sb_ref[c, :, within]
        state_half, back_half = state.astype(BF16), back.astype(BF16)
        y = jnp.where(left, y_two[0], y_two[1]) + nn(r, state_half) * leads
        dx = jnp.where(left, dx_two[0], dx_two[1]) + nn(w, back_half) * tails
        dv_ref[:, at] = dx.astype(BF16)
        dw = dw + nt(vt_ref[:, at], back_half)
        dr = dr + nt(gl_ref[:, at], state_half)
        picks = (iota((N, N), 1) == iota((N, N), 0) // 64 + 2 * i).astype(F32)
        change = change + nn(g.astype(F32) * y - v.astype(F32) * dx, picks, HIGH)
        decays = jnp.where(left_row, bd[:, a : a + 1], bd[:, b : b + 1])
        meet = jnp.sum((decays * state + of_ref[c, :, within]) * back, axis=0, keepdims=True)
        later = later + nn(jnp.broadcast_to(meet, (8, N)), picks, HIGH)[0:1, :]
    half = summed.astype(BF16)
    dw_ref[...] = (dw + tn(half, r)).astype(BF16)
    dr_ref[...] = (dr + nn(half, w)).astype(BF16)
    change = change + jnp.where(iota((T, N), 0) == T - 1, later, 0.0)
    after = (iota((T, T), 0) >= iota((T, T), 1)).astype(F32)
    da_ref[...] = tn(change, after, HIGH)[:HEADS, :]


def vmem(count):
    return [pl.BlockSpec(memory_space=pltpu.VMEM)] * count


def per_device(inputs, out_grad, input_map, output_map, log_decay):
    shape = jax.ShapeDtypeStruct
    states = shape((CORES, N, HALF), F32)
    vt, gl, own_f, own_b, log = pl.pallas_call(
        own,
        out_shape=(shape((T, WIDE), BF16), shape((T, WIDE), BF16), states, states, shape((8, N), F32)),
        in_specs=vmem(5),
        out_specs=tuple(vmem(5)),
        compiler_params=pltpu.CompilerParams(vmem_limit_bytes=LIMIT),
        name="own",
    )(inputs, out_grad, input_map, output_map, log_decay)
    whole = pltpu.VMEM((N, HALF), F32)
    by_z = pltpu.VMEM((Z, SLICE, HALF), F32)
    by_group = pltpu.VMEM((GROUPS, SLICE, HALF), F32)
    dma = pltpu.SemaphoreType.DMA
    state_in, back_in = pl.pallas_call(
        exchange,
        out_shape=(states, states),
        in_specs=vmem(3),
        out_specs=tuple(vmem(2)),
        scratch_shapes=[
            pltpu.VMEM((Z * CORES, 8, N), F32),
            pltpu.VMEM((GROUPS, 8, N), F32),
            *([whole] * 4),
            *([by_z] * 4),
            *([by_group] * 2),
            *([whole] * 6),
            *([pltpu.VMEM((Z, HALF), F32)] * 4),
            pltpu.VMEM((GROUPS, HALF), F32),
            *([dma((GROUPS,))] * 4),
            *([dma((4,))] * 2),
            *([dma((2, Z))] * 2),
            *([dma((2, GROUPS))] * 2),
            *([dma((2, Z))] * 2),
        ],
        compiler_params=pltpu.CompilerParams(
            collective_id=0, has_side_effects=True, vmem_limit_bytes=LIMIT
        ),
        name="exchange",
    )(own_f, own_b, log)
    return pl.pallas_call(
        finish,
        out_shape=(
            shape((T, WIDE), BF16),
            shape((T, N), BF16),
            shape((T, N), BF16),
            shape((HEADS, T), F32),
        ),
        in_specs=vmem(10),
        out_specs=tuple(vmem(4)),
        compiler_params=pltpu.CompilerParams(vmem_limit_bytes=LIMIT),
        name="finish",
    )(inputs, out_grad, input_map, output_map, log_decay, vt, gl, own_f, state_in, back_in)


def solution(mesh):
    tokens = P(("grp", "seq"), None)
    rates = P(None, ("grp", "seq"))
    return jax.shard_map(
        per_device,
        mesh=mesh,
        in_specs=(tokens, tokens, tokens, tokens, rates),
        out_specs=(tokens, tokens, tokens, rates),
        check_vma=False,
    )
```

time: 818 us -> 116 us (0.14)
  waiting for transfers between devices: 389 us -> 0 us
  blocking collectives: 165 us -> 0 us
  other arithmetic: 154 us -> 0 us
  Pallas kernels: 0 us -> 115 us
  matrix products: 48.1 us -> 0 us
  local copies, waits for them, and re-layouts: 42.8 us -> 0 us
  between operations: 14.8 us -> 0.64 us
    all_gather x4 -> x0, waiting for transfers between devices: 274 us -> none  [prefix_2(): pieces = jax.tree.map(lambda part: lax.all_gather(part, axis), value)]
    select_n x90 -> x0, other arithmetic: 141 us -> none  [lap(): jnp.where(position < mine, new, old)]
    pallas_call x0 -> x3, Pallas kernels: none -> 115 us  [the longest x1 91.3 us: per_device(): pl.pallas_call(exchange, out_shape=(states, states), in_specs=vmem(3), ou...]
    psum x1 -> x0, waiting for transfers between devices: 115 us -> none  [per_device(): lax.psum((whole_up[0] * mask_last, whole_up[1] * mask_last, whole_down[0]...]
    unnamed x2 -> x0, blocking collectives: 105 us -> none
    dot_general x24 -> x0, matrix products: 48.1 us -> none  [the longest x5 13.2 us: one_group(): jnp.einsum('hij,jhp->ihp', mixing, group_values, preferred_element_type=j...]
    all_gather x2 -> x0, blocking collectives: 35.6 us -> none  [prefix_2(): pieces = jax.tree.map(lambda part: lax.all_gather(part, axis), value)]
    rev x5 -> x0, local copies, waits for them, and re-layouts: 33.1 us -> none  [the longest x4 33 us: prefix_2(): pieces = jax.tree.map(lambda part: part[::-1], pieces)]
  transfers between devices with their start and end apart: 5 -> 0, of which waited for: 5 -> 0; matrix products, arithmetic and copies ran while one was open for 18% -> 0% of each run, Pallas kernels for 0% -> 0%
where the time goes in v1:
time: 116 us
  Pallas kernels  115 us (99%)
    pallas_call x1, Pallas kernels, per_device(): pl.pallas_call(exchange, out_shape=(states, states), in_specs=vmem(3), ou...  91.3 us
    pallas_call x1, Pallas kernels, per_device(): pl.pallas_call(finish, out_shape=(shape((T, WIDE), BF16), shape((T, N), B...  16.4 us
    pallas_call x1, Pallas kernels, per_device(): pl.pallas_call(own, out_shape=(shape((T, WIDE), BF16), shape((T, WIDE), B...  7.7 us

profile of v1, /device:TPU:1, one launch (start us, length us, event | category | flops | bytes accessed | tf_op | source)
XLA Modules:
  0.0 116.1 jit_solution(1832099048304248147)
XLA Ops:
  0.6 7.7 %own.1 = (bf16[256,2560]{1,0:T(8,128)(2,1)}, bf16[256,2560]{1,0:T(8,128)(2,1)}, f32[2,128,1280]{2,1,0:T(8,128)}, f32[2,128,1280]{2,1,0:T(8,128)}, f32[8,128]{1,0:T(8,128)}) custom-call(bf16[256,2560]{1,0:T(8,128)(2,1)} %v_ref.3, bf16[256,2560]{1,0:T(8,128)(2,1)} %g_ref.3, bf16[256,128]{1,0:T(8,128)(2,1)} %w_ref.3, bf16[256,128]{1,0:T(8,128)(2,1)} %r_ref.3, ...), custom_call_target="tpu_custom_call" | custom-call | tf_op jit(solution)/shard_map/own/pallas_call | solution.py:326
  8.3 91.3 %exchange.1 = (f32[2,128,1280]{2,1,0:T(8,128)}, f32[2,128,1280]{2,1,0:T(8,128)}) custom-call(f32[2,128,1280]{2,1,0:T(8,128)} %get-tuple-element.13.of.of_ref, f32[2,128,1280]{2,1,0:T(8,128)} %get-tuple-element.14.ob, f32[8,128]{1,0:T(8,128)} %get-tuple-element.15.log), custom_call_target="tpu_custom_call" | custom-call | tf_op jit(solution)/shard_map/exchange/pallas_call | solution.py:338
  99.6 16.4 %finish.1 = (bf16[256,2560]{1,0:T(8,128)(2,1)}, bf16[256,128]{1,0:T(8,128)(2,1)}, bf16[256,128]{1,0:T(8,128)(2,1)}, f32[40,256]{1,0:T(8,128)}) custom-call(bf16[256,2560]{1,0:T(8,128)(2,1)} %v_ref.3, bf16[256,2560]{1,0:T(8,128)(2,1)} %g_ref.3, bf16[256,128]{1,0:T(8,128)(2,1)} %w_ref.3, bf16[256,128]{1,0:T(8,128)(2,1)} %r_ref.3, f32[40,256]{1,0:T(8,128)} %a_ref.3, ...), custom_call_target="tpu_custom_call" | custom-call | tf_op jit(solution)/shard_map/finish/pallas_call | solution.py:363

commit v2 on v1

--- a/solution.py
+++ b/solution.py
@@ -16,7 +16,7 @@
 N = 128
 WIDE = 2560
 HALF = WIDE // 2
-Z, CORES, GROUPS = 8, 2, 16
+Z, CORES, GROUPS, SIDE = 8, 2, 16, 4
 SLICE = N // Z
 
 
@@ -71,13 +71,15 @@
 
 def exchange(
     of, ob, log, sf, sb,
-    logs, glogs, xf, xb, cf, cb, uf, ub, pf, pb, tf, tb, df, db, kf, kb, yf, yb,
-    wz, ez, fz, ex, wg,
-    log_s, log_r, glog_s, glog_r, x_s, x_r, u_s, u_r, t_s, t_r, d_s, d_r,
+    logs, glogs, xf, xb, cf, cb, uf, ub, pf, pb, tf, tb, rf, rb, df, db, kf, kb, yf, yb,
+    wz, ez, fz, ex, wg, wr,
+    log_s, log_r, glog_s, glog_r, x_s, x_r, u_s, u_r, t_s, t_r, r_s, r_r, d_s, d_r,
 ):
     g, s = lax.axis_index("grp"), lax.axis_index("seq")
     z, c = s // CORES, s % CORES
-    other = (g, z * CORES + 1 - c)
+    y, x = g // SIDE, g % SIDE
+    partner = z * CORES + 1 - c
+    other = (g, partner)
 
     def copy(src, dst, send, recv, device):
         return pltpu.make_async_remote_copy(
@@ -106,9 +108,8 @@
 
     over(Z * CORES, s, lambda k: greet((g, k)))
     over(GROUPS, g, lambda k: greet((k, s)))
+    logs[s] = log[...]
     pl.semaphore_wait(barrier, Z * CORES - 1 + GROUPS - 1)
-
-    logs[s] = log[...]
 
     def log_copy(k):
         return copy(logs.at[s], logs.at[s], log_s.at[k], log_r.at[s], (g, k))
@@ -116,35 +117,30 @@
     def log_here(k):
         return copy(logs.at[k], logs.at[k], log_s.at[k], log_r.at[k], (g, k))
 
-    over(Z * CORES, s, lambda k: log_copy(k).start())
+    log_copy(partner).start()
     up_f = copy(of.at[1 - c], xf, x_s.at[0], x_r.at[0], other)
     up_b = copy(ob.at[1 - c], xb, x_s.at[1], x_r.at[1], other)
     up_f.start()
     up_b.start()
-    over(Z * CORES, s, lambda k: log_here(k).wait_recv())
-
-    blocks = jnp.max(logs[...], axis=1)
-    glogs[g] = jnp.broadcast_to(jnp.sum(blocks, axis=0, keepdims=True), (8, N))
-
-    def glog_copy(k):
-        return copy(glogs.at[g], glogs.at[g], glog_s.at[k], glog_r.at[g], (k, s))
-
-    def glog_here(k):
-        return copy(glogs.at[k], glogs.at[k], glog_s.at[k], glog_r.at[k], (k, s))
-
-    over(GROUPS, g, lambda k: glog_copy(k).start())
+
+    def over_others(step):
+        def lap(i, carry):
+            step(lax.rem(s - c + CORES + i, Z * CORES))
+            return carry
+
+        lax.fori_loop(0, Z * CORES - CORES, lap, 0)
+
+    over_others(lambda k: log_copy(k).start())
 
     spread = (iota((N, HALF), 0) == iota((N, HALF), 1) // 64 + c * (HEADS // 2)).astype(F32)
-    wide = nn(blocks, spread, HIGH)
-    chip_of, place = iota((Z, Z * CORES), 1) // CORES, iota((Z, Z * CORES), 0)
-    wz[...] = jnp.exp(nn((chip_of == place).astype(F32), wide, HIGH))
-    ez[...] = jnp.exp(nn((chip_of < place).astype(F32), wide, HIGH))
-    fz[...] = jnp.exp(nn((chip_of > place).astype(F32), wide, HIGH))
-    mine = (iota((Z, Z * CORES), 1) == place + z * CORES).astype(F32)
-    ex[...] = jnp.exp(nn(mine, wide, HIGH))
+    is_first = c == 0
+    mine = nn(log[...], spread, HIGH)[0:1, :]
+    log_here(partner).wait_recv()
+    theirs = nn(logs[partner], spread, HIGH)[0:1, :]
+    ex[0:1, :] = jnp.exp(jnp.where(is_first, mine, theirs))
+    ex[1:2, :] = jnp.exp(jnp.where(is_first, theirs, mine))
     first, second = ex[0:1, :], ex[1:2, :]
     one = jnp.ones_like(first)
-    is_first = c == 0
 
     def slices_up(way, own_ref, theirs, chip, up, a, b):
         def put(j):
@@ -165,43 +161,80 @@
     up_b.wait_recv()
     slices_up(1, ob, xb, cb, ub, jnp.where(is_first, one, first), jnp.where(is_first, first, one))
 
+    over_others(lambda k: log_here(k).wait_recv())
+    blocks = jnp.max(logs[...], axis=1)
+    glogs[g] = jnp.broadcast_to(jnp.sum(blocks, axis=0, keepdims=True), (8, N))
+
+    def glog_copy(k):
+        return copy(glogs.at[g], glogs.at[g], glog_s.at[k], glog_r.at[g], (k, s))
+
+    def glog_here(k):
+        return copy(glogs.at[k], glogs.at[k], glog_s.at[k], glog_r.at[k], (k, s))
+
+    over(GROUPS, g, lambda k: glog_copy(k).start())
+    wide = nn(blocks, spread, HIGH)
+    chip_of, place = iota((Z, Z * CORES), 1) // CORES, iota((Z, Z * CORES), 0)
+    wz[...] = jnp.exp(nn((chip_of == place).astype(F32), wide, HIGH))
+    ez[...] = jnp.exp(nn((chip_of < place).astype(F32), wide, HIGH))
+    fz[...] = jnp.exp(nn((chip_of > place).astype(F32), wide, HIGH))
+    over(GROUPS, g, lambda k: glog_here(k).wait_recv())
+    wide = nn(jnp.max(glogs[...], axis=1), spread, HIGH)
+    wg[...] = jnp.exp(wide)
+    row_of, column_of = iota((8, GROUPS), 1) // SIDE, iota((8, GROUPS), 1) % SIDE
+    place = iota((8, GROUPS), 0)
+    beside = ((place == SIDE) & (column_of < x)) | ((place == SIDE + 1) & (column_of > x))
+    picks = ((place < SIDE) & (row_of == place)) | ((row_of == y) & beside)
+    wr[...] = jnp.exp(nn(picks.astype(F32), wide, HIGH))
+
     def up_here(way, chip, up, j):
         return copy(chip.at[rows(j)], up.at[j], u_s.at[way, j], u_r.at[way, j], (g, j * CORES + c))
 
     def total_copy(way, total, k):
-        return copy(total.at[g], total.at[g], t_s.at[way, k], t_r.at[way, g], (k, s))
+        return copy(total.at[x], total.at[x], t_s.at[way, k], t_r.at[way, x], (y * SIDE + k, s))
 
     def total_here(way, total, k):
-        return copy(total.at[k], total.at[k], t_s.at[way, k], t_r.at[way, k], (k, s))
+        return copy(total.at[k], total.at[k], t_s.at[way, k], t_r.at[way, k], (y * SIDE + k, s))
+
+    def row_copy(way, total, k):
+        return copy(total.at[y], total.at[y], r_s.at[way, k], r_r.at[way, y], (k * SIDE + x, s))
+
+    def row_here(way, total, k):
+        return copy(total.at[k], total.at[k], r_s.at[way, k], r_r.at[way, k], (k * SIDE + x, s))
+
+    def down_copy(way, part, down, j):
+        return copy(part.at[j], down.at[rows(z)], d_s.at[way, j], d_r.at[way, z], (g, j * CORES + c))
+
+    def down_here(way, part, down, j):
+        return copy(part.at[j], down.at[rows(j)], d_s.at[way, j], d_r.at[way, j], (g, j * CORES + c))
+
+    empty = jnp.zeros((SLICE, HALF), F32)
 
     def ring(way, chip, up, part, total, order):
         over(Z, z, lambda j: up_here(way, chip, up, j).wait_recv())
-        state = jnp.zeros((SLICE, HALF), F32)
+        state = empty
         for j in order:
             part[j] = state
             state = wz[j : j + 1, :] * state + up[j]
-        total[g] = state
-        over(GROUPS, g, lambda k: total_copy(way, total, k).start())
-
-    ring(0, cf, uf, pf, tf, range(Z))
-    over(GROUPS, g, lambda k: glog_here(k).wait_recv())
-    wg[...] = jnp.exp(nn(jnp.max(glogs[...], axis=1), spread, HIGH))
-    ring(1, cb, ub, pb, tb, range(Z - 1, -1, -1))
-
-    def down_copy(way, part, down, j):
-        return copy(part.at[j], down.at[rows(z)], d_s.at[way, j], d_r.at[way, z], (g, j * CORES + c))
-
-    def down_here(way, part, down, j):
-        return copy(part.at[j], down.at[rows(j)], d_s.at[way, j], d_r.at[way, j], (g, j * CORES + c))
-
-    def groups(way, part, total, down, decay, count, pick):
-        over(GROUPS, g, lambda k: total_here(way, total, k).wait_recv())
-
-        def lap(i, state):
-            k = pick(i)
-            return wg[pl.ds(k, 1), :] * state + total[k]
-
-        state = lax.fori_loop(0, count, lap, jnp.zeros((SLICE, HALF), F32))
+        total[x] = state
+        over(SIDE, x, lambda k: total_copy(way, total, k).start())
+
+    def row(way, total, row_total, order):
+        over(SIDE, x, lambda k: total_here(way, total, k).wait_recv())
+        state, before = empty, empty
+        for k in order:
+            before = jnp.where(k == x, state, before)
+            state = wg[pl.ds(y * SIDE + k, 1), :] * state + total[k]
+        row_total[y] = state
+        over(SIDE, y, lambda k: row_copy(way, row_total, k).start())
+        total[SIDE] = before
+
+    def column(way, part, total, row_total, down, decay, order):
+        over(SIDE, y, lambda k: row_here(way, row_total, k).wait_recv())
+        state, before = empty, empty
+        for k in order:
+            before = jnp.where(k == y, state, before)
+            state = wr[k : k + 1, :] * state + row_total[k]
+        state = wr[SIDE + way : SIDE + way + 1, :] * before + total[SIDE]
 
         def send(j):
             part[j] += decay[pl.ds(j, 1), :] * state
@@ -210,8 +243,13 @@
         over(Z, z, send)
         down[rows(z), :] = part[z] + decay[pl.ds(z, 1), :] * state
 
-    groups(0, pf, tf, df, ez, g, lambda i: i)
-    groups(1, pb, tb, db, fz, GROUPS - 1 - g, lambda i: GROUPS - 1 - i)
+    ahead, back = range(SIDE), range(SIDE - 1, -1, -1)
+    ring(0, cf, uf, pf, tf, range(Z))
+    row(0, tf, rf, ahead)
+    ring(1, cb, ub, pb, tb, range(Z - 1, -1, -1))
+    column(0, pf, tf, rf, df, ez, ahead)
+    row(1, tb, rb, back)
+    column(1, pb, tb, rb, db, fz, back)
 
     over(Z, z, lambda j: down_here(0, pf, df, j).wait_recv())
     out_f = copy(kf, yf, x_s.at[2], x_r.at[2], other)
@@ -250,9 +288,13 @@
 
     over(Z * CORES, s, lambda k: log_copy(k).wait_send())
     over(GROUPS, g, lambda k: glog_copy(k).wait_send())
-    for way, chip, up, part, total, down in ((0, cf, uf, pf, tf, df), (1, cb, ub, pb, tb, db)):
+    for way, chip, up, part, total, row_total, down in (
+        (0, cf, uf, pf, tf, rf, df),
+        (1, cb, ub, pb, tb, rb, db),
+    ):
         over(Z, z, lambda j: up_here(way, chip, up, j).wait_send())
-        over(GROUPS, g, lambda k: total_copy(way, total, k).wait_send())
+        over(SIDE, x, lambda k: total_copy(way, total, k).wait_send())
+        over(SIDE, y, lambda k: row_copy(way, row_total, k).wait_send())
         over(Z, z, lambda j: down_copy(way, part, down, j).wait_send())
     for each in (up_f, up_b, out_f, out_b):
         each.wait_send()
@@ -333,7 +375,7 @@
     )(inputs, out_grad, input_map, output_map, log_decay)
     whole = pltpu.VMEM((N, HALF), F32)
     by_z = pltpu.VMEM((Z, SLICE, HALF), F32)
-    by_group = pltpu.VMEM((GROUPS, SLICE, HALF), F32)
+    by_side = pltpu.VMEM((SIDE + 1, SLICE, HALF), F32)
     dma = pltpu.SemaphoreType.DMA
     state_in, back_in = pl.pallas_call(
         exchange,
@@ -345,14 +387,15 @@
             pltpu.VMEM((GROUPS, 8, N), F32),
             *([whole] * 4),
             *([by_z] * 4),
-            *([by_group] * 2),
+            *([by_side] * 4),
             *([whole] * 6),
             *([pltpu.VMEM((Z, HALF), F32)] * 4),
             pltpu.VMEM((GROUPS, HALF), F32),
+            pltpu.VMEM((8, HALF), F32),
             *([dma((GROUPS,))] * 4),
             *([dma((4,))] * 2),
             *([dma((2, Z))] * 2),
-            *([dma((2, GROUPS))] * 2),
+            *([dma((2, SIDE))] * 4),
             *([dma((2, Z))] * 2),
         ],
         compiler_params=pltpu.CompilerParams(

time: 116 us -> 106 us (0.914)
  Pallas kernels: 115 us -> 105 us
    pallas_call x1, Pallas kernels: 91.3 us -> 80.4 us  [per_device(): pl.pallas_call(exchange, out_shape=(states, states), in_specs=vmem(3), ou...]
where the time goes in v2:
time: 106 us; the launch traced here: 105 us
  Pallas kernels  105 us (99%)
    pallas_call x1, Pallas kernels, per_device(): pl.pallas_call(exchange, out_shape=(states, states), in_specs=vmem(3), ou...  80.4 us
    pallas_call x1, Pallas kernels, per_device(): pl.pallas_call(finish, out_shape=(shape((T, WIDE), BF16), shape((T, N), B...  16.4 us
    pallas_call x1, Pallas kernels, per_device(): pl.pallas_call(own, out_shape=(shape((T, WIDE), BF16), shape((T, WIDE), B...  7.7 us

profile of v2, /device:TPU:1, one launch (start us, length us, event | category | flops | bytes accessed | tf_op | source)
XLA Modules:
  0.0 105.2 jit_solution(3538595889958919163)
XLA Ops:
  0.6 7.7 %own.1 = (bf16[256,2560]{1,0:T(8,128)(2,1)}, bf16[256,2560]{1,0:T(8,128)(2,1)}, f32[2,128,1280]{2,1,0:T(8,128)}, f32[2,128,1280]{2,1,0:T(8,128)}, f32[8,128]{1,0:T(8,128)}) custom-call(bf16[256,2560]{1,0:T(8,128)(2,1)} %v_ref.3, bf16[256,2560]{1,0:T(8,128)(2,1)} %g_ref.3, bf16[256,128]{1,0:T(8,128)(2,1)} %w_ref.3, bf16[256,128]{1,0:T(8,128)(2,1)} %r_ref.3, ...), custom_call_target="tpu_custom_call" | custom-call | tf_op jit(solution)/shard_map/own/pallas_call | solution.py:368
  8.3 80.4 %exchange.1 = (f32[2,128,1280]{2,1,0:T(8,128)}, f32[2,128,1280]{2,1,0:T(8,128)}) custom-call(f32[2,128,1280]{2,1,0:T(8,128)} %get-tuple-element.13.of.of_ref, f32[2,128,1280]{2,1,0:T(8,128)} %get-tuple-element.14.ob, f32[8,128]{1,0:T(8,128)} %get-tuple-element.15.log), custom_call_target="tpu_custom_call" | custom-call | tf_op jit(solution)/shard_map/exchange/pallas_call | solution.py:380
  88.7 16.4 %finish.1 = (bf16[256,2560]{1,0:T(8,128)(2,1)}, bf16[256,128]{1,0:T(8,128)(2,1)}, bf16[256,128]{1,0:T(8,128)(2,1)}, f32[40,256]{1,0:T(8,128)}) custom-call(bf16[256,2560]{1,0:T(8,128)(2,1)} %v_ref.3, bf16[256,2560]{1,0:T(8,128)(2,1)} %g_ref.3, bf16[256,128]{1,0:T(8,128)(2,1)} %w_ref.3, bf16[256,128]{1,0:T(8,128)(2,1)} %r_ref.3, f32[40,256]{1,0:T(8,128)} %a_ref.3, ...), custom_call_target="tpu_custom_call" | custom-call | tf_op jit(solution)/shard_map/finish/pallas_call | solution.py:406

commit v3 on v2

v3 whole, which is shorter than its diff:
```python
import jax
import jax.numpy as jnp
from jax import lax
from jax.experimental import pallas as pl
from jax.experimental.pallas import tpu as pltpu
from jax.sharding import PartitionSpec as P

MESH = pl.DeviceIdType.MESH
HIGH = lax.Precision.HIGHEST
F32 = jnp.float32
BF16 = jnp.bfloat16
LIMIT = 56 * 2**20

T = 256
HEADS = 40
N = 128
WIDE = 2560
HALF = WIDE // 2
Z, CORES, GROUPS, SIDE = 8, 2, 16, 4
SLICE = N // Z
PIECES = 4
CHUNK = 256
CUTS = (14, 16, 18)


def nn(a, b, precision=None):
    return lax.dot_general(
        a, b, (((1,), (0,)), ((), ())), precision=precision, preferred_element_type=F32
    )


def nt(a, b, precision=None):
    return lax.dot_general(
        a, b, (((1,), (1,)), ((), ())), precision=precision, preferred_element_type=F32
    )


def tn(a, b, precision=None):
    return lax.dot_general(
        a, b, (((0,), (0,)), ((), ())), precision=precision, preferred_element_type=F32
    )


def iota(shape, dim):
    return lax.broadcasted_iota(jnp.int32, shape, dim)


def block(
    v_ref, g_ref, w_ref, r_ref, a_ref, dv_ref, dw_ref, dr_ref, da_ref,
    cr, cx, vt, gl, of, ob, yi, di, sm, dw, dr, ch,
    logs, glogs, xf, xb, cf, cb, uf, ub, pf, pb, tf, tb, rf, rb, df, db, kf, kb, sf, sb,
    wz, ez, fz, ex, wg, wr,
    log_s, log_r, glog_s, glog_r, x_s, x_r, u_s, u_r, t_s, t_r, r_s, r_r, d_s, d_r,
):
    g, s = lax.axis_index("grp"), lax.axis_index("seq")
    z, c = s // CORES, s % CORES
    y, x = g // SIDE, g % SIDE
    partner = z * CORES + 1 - c
    other = (g, partner)

    def copy(src, dst, send, recv, device):
        return pltpu.make_async_remote_copy(
            src_ref=src,
            dst_ref=dst,
            send_sem=send,
            recv_sem=recv,
            device_id=device,
            device_id_type=MESH,
        )

    def loop(first, last, step):
        def lap(i, carry):
            step(i)
            return carry

        lax.fori_loop(first, last, lap, 0)

    def over(count, mine, step):
        loop(1, count, lambda i: step(lax.rem(mine + i, count)))

    def over_others(step):
        loop(0, Z * CORES - CORES, lambda i: step(lax.rem(s - c + CORES + i, Z * CORES)))

    def rows(j):
        return pl.ds(pl.multiple_of(j * SLICE, SLICE), SLICE)

    def lanes(start, size):
        return pl.ds(pl.multiple_of(start, N), size)

    barrier = pltpu.get_barrier_semaphore()

    def greet(device):
        pl.semaphore_signal(barrier, inc=1, device_id=device, device_id_type=MESH)

    over(Z * CORES, s, lambda k: greet((g, k)))
    over(GROUPS, g, lambda k: greet((k, s)))

    padded = jnp.concatenate([a_ref[...], jnp.zeros((N - HEADS, T), F32)], axis=0)
    upto = (iota((T, T), 0) <= iota((T, T), 1)).astype(F32)
    cum_rows = nn(padded, upto, HIGH)
    cr[...] = cum_rows
    cum = cum_rows.T
    log = jnp.broadcast_to(cum[T - 1 : T, :], (8, N))
    logs[s] = log
    pl.semaphore_wait(barrier, Z * CORES - 1 + GROUPS - 1)

    def log_copy(k):
        return copy(logs.at[s], logs.at[s], log_s.at[k], log_r.at[s], (g, k))

    def log_here(k):
        return copy(logs.at[k], logs.at[k], log_s.at[k], log_r.at[k], (g, k))

    log_copy(partner).start()
    over_others(lambda k: log_copy(k).start())
    left = iota((T, N), 1) < N // 2
    for i in range(HEADS // 2):
        cx[:, N * i : N * i + N] = jnp.where(left, cum[:, 2 * i : 2 * i + 1], cum[:, 2 * i + 1 : 2 * i + 2])

    def own(half, map_t, token_ref, weighted, state, weight):
        def step(k):
            at = lanes(half * HALF + k * CHUNK, CHUNK)
            part = (token_ref[:, at].astype(F32) * weight(at)).astype(BF16)
            weighted[:, at] = part
            state[half, :, lanes(k * CHUNK, CHUNK)] = nn(map_t, part)

        loop(0, HALF // CHUNK, step)

    def tails(at):
        return jnp.exp(cx[T - 1 : T, at] - cx[:, at])

    def leads(at):
        return jnp.exp(cx[:, at])

    w, r = w_ref[...], r_ref[...]
    w_t, r_t = w.T, r.T
    up_f = copy(of.at[1 - c], xf, x_s.at[0], x_r.at[0], other)
    up_b = copy(ob.at[1 - c], xb, x_s.at[1], x_r.at[1], other)
    own(1 - c, w_t, v_ref, vt, of, tails)
    up_f.start()
    own(c, w_t, v_ref, vt, of, tails)

    spread = (iota((N, HALF), 0) == iota((N, HALF), 1) // 64 + c * (HEADS // 2)).astype(F32)
    is_first = c == 0
    mine = nn(log, spread, HIGH)[0:1, :]
    log_here(partner).wait_recv()
    theirs = nn(logs[partner], spread, HIGH)[0:1, :]
    ex[0:1, :] = jnp.exp(jnp.where(is_first, mine, theirs))
    ex[1:2, :] = jnp.exp(jnp.where(is_first, theirs, mine))
    first, second = ex[0:1, :], ex[1:2, :]
    one = jnp.ones_like(first)

    def slices_up(way, own_ref, theirs, chip, up, a, b):
        def put(j):
            chip[rows(j), :] = a * own_ref[c, rows(j), :] + b * theirs[rows(j), :]

        def send(j):
            put(j)
            copy(chip.at[rows(j)], up.at[z], u_s.at[way, j], u_r.at[way, z], (g, j * CORES + c)).start()

        over(Z, z, send)
        put(z)
        up[z] = chip[rows(z), :]

    up_f.wait_recv()
    slices_up(
        0, of, xf, cf, uf, jnp.where(is_first, second, one), jnp.where(is_first, one, second)
    )

    own(1 - c, r_t, g_ref, gl, ob, leads)
    up_b.start()
    own(c, r_t, g_ref, gl, ob, leads)

    def glog_copy(k):
        return copy(glogs.at[g], glogs.at[g], glog_s.at[k], glog_r.at[g], (k, s))

    def glog_here(k):
        return copy(glogs.at[k], glogs.at[k], glog_s.at[k], glog_r.at[k], (k, s))

    over_others(lambda k: log_here(k).wait_recv())
    blocks = jnp.max(logs[...], axis=1)
    glogs[g] = jnp.broadcast_to(jnp.sum(blocks, axis=0, keepdims=True), (8, N))
    over(GROUPS, g, lambda k: glog_copy(k).start())

    up_b.wait_recv()
    slices_up(1, ob, xb, cb, ub, jnp.where(is_first, one, first), jnp.where(is_first, first, one))

    wide = nn(blocks, spread, HIGH)
    chip_of, place = iota((Z, Z * CORES), 1) // CORES, iota((Z, Z * CORES), 0)
    wz[...] = jnp.exp(nn((chip_of == place).astype(F32), wide, HIGH))
    ez[...] = jnp.exp(nn((chip_of < place).astype(F32), wide, HIGH))
    fz[...] = jnp.exp(nn((chip_of > place).astype(F32), wide, HIGH))
    over(GROUPS, g, lambda k: glog_here(k).wait_recv())
    wide = nn(jnp.max(glogs[...], axis=1), spread, HIGH)
    wg[...] = jnp.exp(wide)
    row_of, column_of = iota((8, GROUPS), 1) // SIDE, iota((8, GROUPS), 1) % SIDE
    place = iota((8, GROUPS), 0)
    beside = ((place == SIDE) & (column_of < x)) | ((place == SIDE + 1) & (column_of > x))
    picks = ((place < SIDE) & (row_of == place)) | ((row_of == y) & beside)
    wr[...] = jnp.exp(nn(picks.astype(F32), wide, HIGH))

    causal = iota((T, T), 0) >= iota((T, T), 1)
    scores = nt(r, w)
    sm[...] = jnp.zeros((T, T), F32)

    def intra(i):
        at = lanes(i * N, N)
        v, gr, two = v_ref[:, at], g_ref[:, at], cx[:, at]
        y_two, dx_two = [], []
        total = sm[...]
        for k in range(2):
            gap = two[:, 64 * k : 64 * k + 1] - cr[pl.ds(2 * i + k, 1), :]
            decay = jnp.exp(jnp.where(causal, gap, -jnp.inf))
            mixing = (scores * decay).astype(BF16)
            y_two.append(nn(mixing, v))
            dx_two.append(tn(mixing, gr))
            head = jnp.where(left if k == 0 else jnp.logical_not(left), gr, jnp.zeros_like(gr))
            total = total + nt(head, v) * decay
        sm[...] = total
        yi[:, at] = jnp.where(left, y_two[0], y_two[1])
        di[:, at] = jnp.where(left, dx_two[0], dx_two[1])

    loop(0, CUTS[0], intra)

    def up_here(way, chip, up, j):
        return copy(chip.at[rows(j)], up.at[j], u_s.at[way, j], u_r.at[way, j], (g, j * CORES + c))

    def total_copy(way, total, k):
        return copy(total.at[x], total.at[x], t_s.at[way, k], t_r.at[way, x], (y * SIDE + k, s))

    def total_here(way, total, k):
        return copy(total.at[k], total.at[k], t_s.at[way, k], t_r.at[way, k], (y * SIDE + k, s))

    def row_copy(way, total, k):
        return copy(total.at[y], total.at[y], r_s.at[way, k], r_r.at[way, y], (k * SIDE + x, s))

    def row_here(way, total, k):
        return copy(total.at[k], total.at[k], r_s.at[way, k], r_r.at[way, k], (k * SIDE + x, s))

    def down_copy(way, part, down, j):
        return copy(part.at[j], down.at[rows(z)], d_s.at[way, j], d_r.at[way, z], (g, j * CORES + c))

    def down_here(way, part, down, j):
        return copy(part.at[j], down.at[rows(j)], d_s.at[way, j], d_r.at[way, j], (g, j * CORES + c))

    empty = jnp.zeros((SLICE, HALF), F32)

    def ring(way, chip, up, part, total, order):
        over(Z, z, lambda j: up_here(way, chip, up, j).wait_recv())
        state = empty
        for j in order:
            part[j] = state
            state = wz[j : j + 1, :] * state + up[j]
        total[x] = state
        over(SIDE, x, lambda k: total_copy(way, total, k).start())

    def row(way, total, row_total, order):
        over(SIDE, x, lambda k: total_here(way, total, k).wait_recv())
        state, before = empty, empty
        for k in order:
            before = jnp.where(k == x, state, before)
            state = wg[pl.ds(y * SIDE + k, 1), :] * state + total[k]
        row_total[y] = state
        over(SIDE, y, lambda k: row_copy(way, row_total, k).start())
        total[SIDE] = before

    def column(way, part, total, row_total, down, decay, order):
        over(SIDE, y, lambda k: row_here(way, row_total, k).wait_recv())
        state, before = empty, empty
        for k in order:
            before = jnp.where(k == y, state, before)
            state = wr[k : k + 1, :] * state + row_total[k]
        state = wr[SIDE + way : SIDE + way + 1, :] * before + total[SIDE]

        def send(j):
            part[j] += decay[pl.ds(j, 1), :] * state
            down_copy(way, part, down, j).start()

        over(Z, z, send)
        down[rows(z), :] = part[z] + decay[pl.ds(z, 1), :] * state

    ahead, back = range(SIDE), range(SIDE - 1, -1, -1)
    ring(0, cf, uf, pf, tf, range(Z))
    loop(CUTS[0], CUTS[1], intra)
    row(0, tf, rf, ahead)
    loop(CUTS[1], CUTS[2], intra)
    ring(1, cb, ub, pb, tb, range(Z - 1, -1, -1))
    column(0, pf, tf, rf, df, ez, ahead)
    loop(CUTS[2], HEADS // 2, intra)
    row(1, tb, rb, back)
    half = sm[...].astype(BF16)
    dw[...] = tn(half, r)
    dr[...] = nn(half, w)
    column(1, pb, tb, rb, db, fz, back)

    def finish_f(side):
        def step(k):
            at, within = lanes(side * HALF + k * CHUNK, CHUNK), lanes(k * CHUNK, CHUNK)
            state = sf[side, :, within]
            state_half = state.astype(BF16)
            full = yi[:, at] + nn(r, state_half) * leads(at)
            yi[:, at] = g_ref[:, at].astype(F32) * full
            dr[...] += nt(gl[:, at], state_half)
            sf[side, :, within] = jnp.exp(cx[T - 1 : T, at]) * state + of[side, :, within]

        loop(0, HALF // CHUNK, step)

    last = iota((T, CHUNK), 0) == T - 1
    ch[...] = jnp.zeros((T, N), F32)

    def finish_b(side):
        def step(k):
            at, within = lanes(side * HALF + k * CHUNK, CHUNK), lanes(k * CHUNK, CHUNK)
            back_in = sb[side, :, within]
            back_half = back_in.astype(BF16)
            full = di[:, at] + nn(w, back_half) * tails(at)
            dv_ref[:, at] = full.astype(BF16)
            dw[...] += nt(vt[:, at], back_half)
            meet = jnp.sum(sf[side, :, within] * back_in, axis=0, keepdims=True)
            change = yi[:, at] - v_ref[:, at].astype(F32) * full + jnp.where(last, meet, 0.0)
            high = change.astype(BF16)
            low = (change - high.astype(F32)).astype(BF16)
            head = (side * HALF + k * CHUNK) // 64 + iota((CHUNK, N), 0) // 64
            picks = (iota((CHUNK, N), 1) == head).astype(F32).astype(BF16)
            ch[...] += nn(high, picks) + nn(low, picks)

        loop(0, HALF // CHUNK, step)

    over(Z, z, lambda j: down_here(0, pf, df, j).wait_recv())
    out_f = copy(kf, sf.at[c], x_s.at[2], x_r.at[2], other)

    @pl.when(is_first)
    def _():
        kf[...] = first * df[...] + of[c]
        sf[c] = df[...]

    @pl.when(jnp.logical_not(is_first))
    def _():
        kf[...] = df[...]
        sf[c] = first * df[...] + xf[...]

    out_f.start()
    finish_f(c)
    out_f.wait_recv()
    finish_f(1 - c)

    over(Z, z, lambda j: down_here(1, pb, db, j).wait_recv())
    out_b = copy(kb, sb.at[c], x_s.at[3], x_r.at[3], other)

    @pl.when(is_first)
    def _():
        kb[...] = db[...]
        sb[c] = second * db[...] + xb[...]

    @pl.when(jnp.logical_not(is_first))
    def _():
        kb[...] = second * db[...] + ob[c]
        sb[c] = db[...]

    out_b.start()
    finish_b(c)
    out_b.wait_recv()
    finish_b(1 - c)
    dw_ref[...] = dw[...].astype(BF16)
    dr_ref[...] = dr[...].astype(BF16)
    after = (iota((T, T), 0) >= iota((T, T), 1)).astype(F32)
    da_ref[...] = tn(ch[...], after, HIGH)[:HEADS, :]

    over(Z * CORES, s, lambda k: log_copy(k).wait_send())
    over(GROUPS, g, lambda k: glog_copy(k).wait_send())
    for way, chip, up, part, total, row_total, down in (
        (0, cf, uf, pf, tf, rf, df),
        (1, cb, ub, pb, tb, rb, db),
    ):
        over(Z, z, lambda j: up_here(way, chip, up, j).wait_send())
        over(SIDE, x, lambda k: total_copy(way, total, k).wait_send())
        over(SIDE, y, lambda k: row_copy(way, row_total, k).wait_send())
        over(Z, z, lambda j: down_copy(way, part, down, j).wait_send())
    for each in (up_f, up_b, out_f, out_b):
        each.wait_send()


def deliver(dv_in, dw_in, dr_in, da_in, dv_ref, dw_ref, dr_ref, da_ref, dv, dw, dr, da, sem):
    step = T // PIECES
    pieces = [pl.ds(i * step, step) for i in range(PIECES)]
    ways = [(dv_in.at[at], dv.at[at], dv_ref.at[at]) for at in pieces]
    ways += [(dw_in, dw, dw_ref), (dr_in, dr, dr_ref), (da_in, da, da_ref)]
    inward = [pltpu.make_async_copy(a, b, sem.at[0, i]) for i, (a, b, _) in enumerate(ways)]
    outward = [pltpu.make_async_copy(b, c, sem.at[1, i]) for i, (_, b, c) in enumerate(ways)]
    for each in inward:
        each.start()
    for one, two in zip(inward, outward):
        one.wait()
        two.start()
    for each in outward:
        each.wait()


def vmem(count):
    return [pl.BlockSpec(memory_space=pltpu.VMEM)] * count


def per_device(inputs, out_grad, input_map, output_map, log_decay):
    shape = jax.ShapeDtypeStruct
    whole = pltpu.VMEM((N, HALF), F32)
    both = pltpu.VMEM((CORES, N, HALF), F32)
    by_z = pltpu.VMEM((Z, SLICE, HALF), F32)
    by_side = pltpu.VMEM((SIDE + 1, SLICE, HALF), F32)
    dma = pltpu.SemaphoreType.DMA
    outs = (
        shape((T, WIDE), BF16),
        shape((T, N), BF16),
        shape((T, N), BF16),
        shape((HEADS, T), F32),
    )
    made = pl.pallas_call(
        block,
        out_shape=outs,
        in_specs=vmem(5),
        out_specs=tuple(vmem(4)),
        scratch_shapes=[
            pltpu.VMEM((N, T), F32),
            pltpu.VMEM((T, WIDE), F32),
            *([pltpu.VMEM((T, WIDE), BF16)] * 2),
            *([both] * 2),
            *([pltpu.VMEM((T, WIDE), F32)] * 2),
            pltpu.VMEM((T, T), F32),
            *([pltpu.VMEM((T, N), F32)] * 3),
            pltpu.VMEM((Z * CORES, 8, N), F32),
            pltpu.VMEM((GROUPS, 8, N), F32),
            *([whole] * 4),
            *([by_z] * 4),
            *([by_side] * 4),
            *([whole] * 4),
            *([both] * 2),
            *([pltpu.VMEM((Z, HALF), F32)] * 4),
            pltpu.VMEM((GROUPS, HALF), F32),
            pltpu.VMEM((8, HALF), F32),
            *([dma((GROUPS,))] * 4),
            *([dma((4,))] * 2),
            *([dma((2, Z))] * 2),
            *([dma((2, SIDE))] * 4),
            *([dma((2, Z))] * 2),
        ],
        compiler_params=pltpu.CompilerParams(
            collective_id=0, has_side_effects=True, vmem_limit_bytes=LIMIT
        ),
        name="block",
    )(inputs, out_grad, input_map, output_map, log_decay)
    anywhere = [pl.BlockSpec(memory_space=pl.ANY)] * 4
    return pl.pallas_call(
        deliver,
        out_shape=outs,
        in_specs=anywhere,
        out_specs=tuple(anywhere),
        scratch_shapes=[*(pltpu.VMEM(o.shape, o.dtype) for o in outs), dma((2, PIECES + 3))],
        compiler_params=pltpu.CompilerParams(vmem_limit_bytes=LIMIT),
        name="deliver",
    )(*made)


def solution(mesh):
    tokens = P(("grp", "seq"), None)
    rates = P(None, ("grp", "seq"))
    return jax.shard_map(
        per_device,
        mesh=mesh,
        in_specs=(tokens, tokens, tokens, tokens, rates),
        out_specs=(tokens, tokens, tokens, rates),
        check_vma=False,
    )
```

time: 106 us -> 87.6 us (0.83)
  Pallas kernels: 105 us -> 86.8 us
    pallas_call x3 -> x2, Pallas kernels: 105 us -> 86.8 us  [the longest x1 84.6 us: per_device(): pl.pallas_call(block, out_shape=outs, in_specs=vmem(5), out_specs=tuple(v...]
where the time goes in v3:
time: 87.6 us; the launch traced here: 87.4 us
  Pallas kernels  86.8 us (99%)
    pallas_call x1, Pallas kernels, per_device(): pl.pallas_call(block, out_shape=outs, in_specs=vmem(5), out_specs=tuple(v...  84.6 us
    pallas_call x1, Pallas kernels, per_device(): pl.pallas_call(deliver, out_shape=outs, in_specs=anywhere, out_specs=tupl...  2.19 us

profile of v3, /device:TPU:1, one launch (start us, length us, event | category | flops | bytes accessed | tf_op | source)
XLA Modules:
  0.0 87.4 jit_solution(10617921275827071359)
XLA Ops:
  0.6 84.6 %block.1 = (bf16[256,2560]{1,0:T(8,128)(2,1)}, bf16[256,128]{1,0:T(8,128)(2,1)}, bf16[256,128]{1,0:T(8,128)(2,1)}, f32[40,256]{1,0:T(8,128)}) custom-call(bf16[256,2560]{1,0:T(8,128)(2,1)} %v_ref.1, bf16[256,2560]{1,0:T(8,128)(2,1)} %g_ref.1, bf16[256,128]{1,0:T(8,128)(2,1)} %w_ref.1, bf16[256,128]{1,0:T(8,128)(2,1)} %r_ref.1, f32[40,256]{1,0:T(8,128)} %a_ref.1), custom_call_target="tpu_custom_call" | custom-call | tf_op jit(solution)/shard_map/block/pallas_call | solution.py:415
  85.2 2.2 %deliver.1 = (bf16[256,2560]{1,0:T(8,128)(2,1)}, bf16[256,128]{1,0:T(8,128)(2,1)}, bf16[256,128]{1,0:T(8,128)(2,1)}, f32[40,256]{1,0:T(8,128)}) custom-call(bf16[256,2560]{1,0:T(8,128)(2,1)} %get-tuple-element.8.dv_in, bf16[256,128]{1,0:T(8,128)(2,1)} %get-tuple-element.9.dw_in, bf16[256,128]{1,0:T(8,128)(2,1)} %get-tuple-element.10.dr_in, ...), custom_call_target="tpu_custom_call" | custom-call | tf_op jit(solution)/shard_map/deliver/pallas_call | solution.py:450

commit v4 on v3

--- a/solution.py
+++ b/solution.py
@@ -50,7 +50,7 @@
     cr, cx, vt, gl, of, ob, yi, di, sm, dw, dr, ch,
     logs, glogs, xf, xb, cf, cb, uf, ub, pf, pb, tf, tb, rf, rb, df, db, kf, kb, sf, sb,
     wz, ez, fz, ex, wg, wr,
-    log_s, log_r, glog_s, glog_r, x_s, x_r, u_s, u_r, t_s, t_r, r_s, r_r, d_s, d_r,
+    log_s, log_r, glog_s, glog_r, x_s, x_r, h_s, h_r, u_s, u_r, t_s, t_r, r_s, r_r, d_s, d_r,
 ):
     g, s = lax.axis_index("grp"), lax.axis_index("seq")
     z, c = s // CORES, s % CORES
@@ -102,7 +102,6 @@
     cum = cum_rows.T
     log = jnp.broadcast_to(cum[T - 1 : T, :], (8, N))
     logs[s] = log
-    pl.semaphore_wait(barrier, Z * CORES - 1 + GROUPS - 1)
 
     def log_copy(k):
         return copy(logs.at[s], logs.at[s], log_s.at[k], log_r.at[s], (g, k))
@@ -110,8 +109,6 @@
     def log_here(k):
         return copy(logs.at[k], logs.at[k], log_s.at[k], log_r.at[k], (g, k))
 
-    log_copy(partner).start()
-    over_others(lambda k: log_copy(k).start())
     left = iota((T, N), 1) < N // 2
     for i in range(HEADS // 2):
         cx[:, N * i : N * i + N] = jnp.where(left, cum[:, 2 * i : 2 * i + 1], cum[:, 2 * i + 1 : 2 * i + 2])
@@ -133,11 +130,19 @@
 
     w, r = w_ref[...], r_ref[...]
     w_t, r_t = w.T, r.T
-    up_f = copy(of.at[1 - c], xf, x_s.at[0], x_r.at[0], other)
-    up_b = copy(ob.at[1 - c], xb, x_s.at[1], x_r.at[1], other)
+
+    def half_copy(way, own_ref, theirs, j):
+        return copy(own_ref.at[1 - c, rows(j)], theirs.at[rows(j)], h_s.at[way, j], h_r.at[way, j], other)
+
+    def half_up(way, own_ref, theirs):
+        loop(1, Z + 1, lambda i: half_copy(way, own_ref, theirs, lax.rem(z + i, Z)).start())
+
     own(1 - c, w_t, v_ref, vt, of, tails)
-    up_f.start()
     own(c, w_t, v_ref, vt, of, tails)
+    pl.semaphore_wait(barrier, Z * CORES - 1 + GROUPS - 1)
+    log_copy(partner).start()
+    half_up(0, of, xf)
+    over_others(lambda k: log_copy(k).start())
 
     spread = (iota((N, HALF), 0) == iota((N, HALF), 1) // 64 + c * (HEADS // 2)).astype(F32)
     is_first = c == 0
@@ -151,6 +156,7 @@
 
     def slices_up(way, own_ref, theirs, chip, up, a, b):
         def put(j):
+            half_copy(way, own_ref, theirs, j).wait_recv()
             chip[rows(j), :] = a * own_ref[c, rows(j), :] + b * theirs[rows(j), :]
 
         def send(j):
@@ -161,13 +167,12 @@
         put(z)
         up[z] = chip[rows(z), :]
 
-    up_f.wait_recv()
     slices_up(
         0, of, xf, cf, uf, jnp.where(is_first, second, one), jnp.where(is_first, one, second)
     )
 
     own(1 - c, r_t, g_ref, gl, ob, leads)
-    up_b.start()
+    half_up(1, ob, xb)
     own(c, r_t, g_ref, gl, ob, leads)
 
     def glog_copy(k):
@@ -181,7 +186,6 @@
     glogs[g] = jnp.broadcast_to(jnp.sum(blocks, axis=0, keepdims=True), (8, N))
     over(GROUPS, g, lambda k: glog_copy(k).start())
 
-    up_b.wait_recv()
     slices_up(1, ob, xb, cb, ub, jnp.where(is_first, one, first), jnp.where(is_first, first, one))
 
     wide = nn(blocks, spread, HIGH)
@@ -326,7 +330,7 @@
         loop(0, HALF // CHUNK, step)
 
     over(Z, z, lambda j: down_here(0, pf, df, j).wait_recv())
-    out_f = copy(kf, sf.at[c], x_s.at[2], x_r.at[2], other)
+    out_f = copy(kf, sf.at[c], x_s.at[0], x_r.at[0], other)
 
     @pl.when(is_first)
     def _():
@@ -344,7 +348,7 @@
     finish_f(1 - c)
 
     over(Z, z, lambda j: down_here(1, pb, db, j).wait_recv())
-    out_b = copy(kb, sb.at[c], x_s.at[3], x_r.at[3], other)
+    out_b = copy(kb, sb.at[c], x_s.at[1], x_r.at[1], other)
 
     @pl.when(is_first)
     def _():
@@ -375,8 +379,10 @@
         over(SIDE, x, lambda k: total_copy(way, total, k).wait_send())
         over(SIDE, y, lambda k: row_copy(way, row_total, k).wait_send())
         over(Z, z, lambda j: down_copy(way, part, down, j).wait_send())
-    for each in (up_f, up_b, out_f, out_b):
-        each.wait_send()
+    for way, own_ref, theirs in ((0, of, xf), (1, ob, xb)):
+        loop(0, Z, lambda j: half_copy(way, own_ref, theirs, j).wait_send())
+    out_f.wait_send()
+    out_b.wait_send()
 
 
 def deliver(dv_in, dw_in, dr_in, da_in, dv_ref, dw_ref, dr_ref, da_ref, dv, dw, dr, da, sem):
@@ -436,8 +442,8 @@
             pltpu.VMEM((GROUPS, HALF), F32),
             pltpu.VMEM((8, HALF), F32),
             *([dma((GROUPS,))] * 4),
-            *([dma((4,))] * 2),
-            *([dma((2, Z))] * 2),
+            *([dma((2,))] * 2),
+            *([dma((2, Z))] * 4),
             *([dma((2, SIDE))] * 4),
             *([dma((2, Z))] * 2),
         ],

time: 87.6 us -> 85.6 us (0.977)
  Pallas kernels: 86.8 us -> 84.8 us
    pallas_call x1, Pallas kernels: 84.6 us -> 82.6 us  [per_device(): pl.pallas_call(block, out_shape=outs, in_specs=vmem(5), out_specs=tuple(v...]
where the time goes in v4:
time: 85.6 us; the launch traced here: 85.4 us
  Pallas kernels  84.8 us (99%)
    pallas_call x1, Pallas kernels, per_device(): pl.pallas_call(block, out_shape=outs, in_specs=vmem(5), out_specs=tuple(v...  82.6 us
    pallas_call x1, Pallas kernels, per_device(): pl.pallas_call(deliver, out_shape=outs, in_specs=anywhere, out_specs=tupl...  2.19 us

profile of v4, /device:TPU:1, one launch (start us, length us, event | category | flops | bytes accessed | tf_op | source)
XLA Modules:
  0.0 85.4 jit_solution(2358178732478746549)
XLA Ops:
  0.6 82.6 %block.1 = (bf16[256,2560]{1,0:T(8,128)(2,1)}, bf16[256,128]{1,0:T(8,128)(2,1)}, bf16[256,128]{1,0:T(8,128)(2,1)}, f32[40,256]{1,0:T(8,128)}) custom-call(bf16[256,2560]{1,0:T(8,128)(2,1)} %v_ref.1, bf16[256,2560]{1,0:T(8,128)(2,1)} %g_ref.1, bf16[256,128]{1,0:T(8,128)(2,1)} %w_ref.1, bf16[256,128]{1,0:T(8,128)(2,1)} %r_ref.1, f32[40,256]{1,0:T(8,128)} %a_ref.1), custom_call_target="tpu_custom_call" | custom-call | tf_op jit(solution)/shard_map/block/pallas_call | solution.py:421
  83.2 2.2 %deliver.1 = (bf16[256,2560]{1,0:T(8,128)(2,1)}, bf16[256,128]{1,0:T(8,128)(2,1)}, bf16[256,128]{1,0:T(8,128)(2,1)}, f32[40,256]{1,0:T(8,128)}) custom-call(bf16[256,2560]{1,0:T(8,128)(2,1)} %get-tuple-element.8.dv_in, bf16[256,128]{1,0:T(8,128)(2,1)} %get-tuple-element.9.dw_in, bf16[256,128]{1,0:T(8,128)(2,1)} %get-tuple-element.10.dr_in, ...), custom_call_target="tpu_custom_call" | custom-call | tf_op jit(solution)/shard_map/deliver/pallas_call | solution.py:456

commit v5 on v4

--- a/solution.py
+++ b/solution.py
@@ -46,8 +46,8 @@
 
 
 def block(
-    v_ref, g_ref, w_ref, r_ref, a_ref, dv_ref, dw_ref, dr_ref, da_ref,
-    cr, cx, vt, gl, of, ob, yi, di, sm, dw, dr, ch,
+    v_in, g_in, w_in, r_in, a_in, dv_ref, dw_ref, dr_ref, da_ref,
+    v_ref, g_ref, w_ref, r_ref, a_ref, in_s, cr, cx, vt, gl, of, ob, yi, di, sm, dw, dr, ch,
     logs, glogs, xf, xb, cf, cb, uf, ub, pf, pb, tf, tb, rf, rb, df, db, kf, kb, sf, sb,
     wz, ez, fz, ex, wg, wr,
     log_s, log_r, glog_s, glog_r, x_s, x_r, h_s, h_r, u_s, u_r, t_s, t_r, r_s, r_r, d_s, d_r,
@@ -94,6 +94,11 @@
 
     over(Z * CORES, s, lambda k: greet((g, k)))
     over(GROUPS, g, lambda k: greet((k, s)))
+    arrays = ((a_in, a_ref), (v_in, v_ref), (w_in, w_ref), (r_in, r_ref), (g_in, g_ref))
+    loads = [pltpu.make_async_copy(far, near, in_s.at[i]) for i, (far, near) in enumerate(arrays)]
+    for each in loads:
+        each.start()
+    loads[0].wait()
 
     padded = jnp.concatenate([a_ref[...], jnp.zeros((N - HEADS, T), F32)], axis=0)
     upto = (iota((T, T), 0) <= iota((T, T), 1)).astype(F32)
@@ -128,6 +133,8 @@
     def leads(at):
         return jnp.exp(cx[:, at])
 
+    for each in loads[1:]:
+        each.wait()
     w, r = w_ref[...], r_ref[...]
     w_t, r_t = w.T, r.T
 
@@ -421,9 +428,13 @@
     made = pl.pallas_call(
         block,
         out_shape=outs,
-        in_specs=vmem(5),
+        in_specs=[pl.BlockSpec(memory_space=pl.ANY)] * 5,
         out_specs=tuple(vmem(4)),
         scratch_shapes=[
+            *([pltpu.VMEM((T, WIDE), BF16)] * 2),
+            *([pltpu.VMEM((T, N), BF16)] * 2),
+            pltpu.VMEM((HEADS, T), F32),
+            dma((5,)),
             pltpu.VMEM((N, T), F32),
             pltpu.VMEM((T, WIDE), F32),
             *([pltpu.VMEM((T, WIDE), BF16)] * 2),

time: 85.6 us -> 84.1 us (0.982)
  Pallas kernels: 84.8 us -> 83.3 us
    pallas_call x1, Pallas kernels: 82.6 us -> 81.1 us  [per_device(): pl.pallas_call(block, out_shape=outs, in_specs=[pl.BlockSpec(memory_space...]
where the time goes in v5:
time: 84.1 us; the launch traced here: 83.9 us
  Pallas kernels  83.3 us (99%)
    pallas_call x1, Pallas kernels, per_device(): pl.pallas_call(block, out_shape=outs, in_specs=[pl.BlockSpec(memory_space...  81.1 us
    pallas_call x1, Pallas kernels, per_device(): pl.pallas_call(deliver, out_shape=outs, in_specs=anywhere, out_specs=tupl...  2.19 us

profile of v5, /device:TPU:1, one launch (start us, length us, event | category | flops | bytes accessed | tf_op | source)
XLA Modules:
  0.0 83.9 jit_solution(12694942988825032667)
XLA Ops:
  0.6 81.1 %block.1 = (bf16[256,2560]{1,0:T(8,128)(2,1)}, bf16[256,128]{1,0:T(8,128)(2,1)}, bf16[256,128]{1,0:T(8,128)(2,1)}, f32[40,256]{1,0:T(8,128)}) custom-call(bf16[256,2560]{1,0:T(8,128)(2,1)} %v_in.1, bf16[256,2560]{1,0:T(8,128)(2,1)} %g_in.1, bf16[256,128]{1,0:T(8,128)(2,1)} %w_in.1, bf16[256,128]{1,0:T(8,128)(2,1)} %r_in.1, f32[40,256]{1,0:T(8,128)} %a_in.1), custom_call_target="tpu_custom_call" | custom-call | tf_op jit(solution)/shard_map/block/pallas_call | solution.py:428
  81.8 2.2 %deliver.1 = (bf16[256,2560]{1,0:T(8,128)(2,1)}, bf16[256,128]{1,0:T(8,128)(2,1)}, bf16[256,128]{1,0:T(8,128)(2,1)}, f32[40,256]{1,0:T(8,128)}) custom-call(bf16[256,2560]{1,0:T(8,128)(2,1)} %get-tuple-element.8.dv_in, bf16[256,128]{1,0:T(8,128)(2,1)} %get-tuple-element.9.dw_in, bf16[256,128]{1,0:T(8,128)(2,1)} %get-tuple-element.10.dr_in, ...), custom_call_target="tpu_custom_call" | custom-call | tf_op jit(solution)/shard_map/deliver/pallas_call | solution.py:467
